TPU v7x, 32 devices: a whole 2x2x4 slice. The times are simulated.
32 devices in a mesh: dp: 8 (over z, x), seq: 4 (over y, core).
Axes of the slice: x: 2, y: 2, z: 4, core: 2. Of those that a mesh axis runs over, the one named last changes fastest.
Arguments:
- dec_states: bfloat16 [8, 1024, 768], P('dp', 'seq'), may hold values from -6 to 6
- enc_states: bfloat16 [8, 1024, 768], P('dp', 'seq'), may hold values from -6 to 6
- out_grad: bfloat16 [8, 1024, 768], P('dp', 'seq'), may hold values from -6 to 6
- dec_lengths: int32 [8, 4], P('dp'), may hold values from 1 to 1021, as said below
- enc_lengths: int32 [8, 4], P('dp'), may hold values from 1 to 1021, as said below
- self_query: bfloat16 [768, 768], replicated, may hold values from -0.109375 to 0.109375
- self_key: bfloat16 [768, 768], replicated, may hold values from -0.109375 to 0.109375
- self_value: bfloat16 [768, 768], replicated, may hold values from -0.21875 to 0.21875
- self_output: bfloat16 [768, 768], replicated, may hold values from -1.25 to 1.25
- cross_query: bfloat16 [768, 768], replicated, may hold values from -0.109375 to 0.109375
- cross_key: bfloat16 [768, 768], replicated, may hold values from -0.109375 to 0.109375
- cross_value: bfloat16 [768, 768], replicated, may hold values from -0.21875 to 0.21875
- cross_output: bfloat16 [768, 768], replicated, may hold values from -1.25 to 1.25
- ffn_in: bfloat16 [768, 3072], replicated, may hold values from -0.21875 to 0.21875
- ffn_out: bfloat16 [3072, 768], replicated, may hold values from -0.109375 to 0.109375
- gain_self: bfloat16 [768], replicated, may hold values from 0.099609375 to 1.8984375
- gain_cross: bfloat16 [768], replicated, may hold values from 0.099609375 to 1.8984375
- gain_ffn: bfloat16 [768], replicated, may hold values from 0.099609375 to 1.8984375
- position_bias: bfloat16 [32, 12], replicated, may hold values from -4 to 4
Outputs:
- layer_out: bfloat16 [8, 1024, 768], P('dp', 'seq')
- dec_grad: float32 [8, 1024, 768], P('dp', 'seq')
- enc_grad: float32 [8, 1024, 768], P('dp', 'seq')
- grad_self_query: float32 [768, 768], P('seq')
- grad_self_key: float32 [768, 768], P('seq')
- grad_self_value: float32 [768, 768], P('seq')
- grad_self_output: float32 [768, 768], P('seq')
- grad_cross_query: float32 [768, 768], P('seq')
- grad_cross_key: float32 [768, 768], P('seq')
- grad_cross_value: float32 [768, 768], P('seq')
- grad_cross_output: float32 [768, 768], P('seq')
- grad_ffn_in: float32 [768, 3072], P('seq')
- grad_ffn_out: float32 [3072, 768], P('seq')
- grad_gain_self: float32 [768], P('seq')
- grad_gain_cross: float32 [768], P('seq')
- grad_gain_ffn: float32 [768], P('seq')
- grad_position_bias: float32 [32, 12], P('seq')
Inputs may be any that keep to these rules, and one draw needn't show every extreme that they name: `dec_lengths`: the 4 lengths of a row sum to 1024. In every row one item, the second or third, begins within the first 256 positions and ends within the last 256; each other item is shorter than 128. In one row of every draw the other items have length 1 each. `enc_lengths`: as for dec_lengths, drawn apart from them.
All inputs are finite; a program needn't handle non-finite values.
Results may differ from a plain program's by a relative error of at most 0.028.
The roundings to bfloat16 on the way count: a program that leaves them out, or rounds other values in their place, can miss the bound.
Values may be sent and summed in bfloat16 or wider, within the bound.
A program may use at most 192 MiB of HBM per device.

v0:
```python
import functools
import math
from types import SimpleNamespace

import jax
import jax.numpy as jnp
from jax import lax
from jax.experimental import pallas as pl
from jax.experimental.pallas import tpu as pltpu
from jax.sharding import PartitionSpec as P

MESH = pl.DeviceIdType.MESH
EPS = 1e-06
NEG = -1000000000.0
NEAR = 128
F32 = jnp.float32
LOW = jnp.bfloat16


def dot(left, right):
    return jnp.dot(left, right, preferred_element_type=F32)


def dot_nt(left, right):
    return lax.dot_general(left, right, (((1,), (1,)), ((), ())), preferred_element_type=F32)


def add_low(left, right):
    return (left.astype(F32) + right.astype(F32)).astype(LOW)


def block(index, size):
    return pl.ds(pl.multiple_of(index * size, size), size)


def bucket_of(distance):
    farther = jnp.full(distance.shape, 16, jnp.int32)
    for level in range(1, 16):
        farther = farther + (distance >= math.ceil(16 * 8 ** (level / 16))).astype(jnp.int32)
    return jnp.where(distance < 16, distance, farther)


def bucket_terms(buckets):
    shape = (buckets, 2 * NEAR)
    lanes = lax.broadcasted_iota(jnp.int32, shape, 1)
    return (bucket_of(lanes) == lax.broadcasted_iota(jnp.int32, shape, 0)).astype(F32)


def scale_of(values):
    return lax.rsqrt(jnp.mean(values * values, axis=-1, keepdims=True) + EPS)


def norm_back(values, gain, grad):
    scale = scale_of(values)
    gain_grad = jnp.sum(grad * values * scale, axis=0, keepdims=True)
    inner = jnp.mean(values * gain * grad, axis=-1, keepdims=True)
    return scale * gain * grad - values * (scale * scale * scale) * inner, gain_grad


def head_blocks(pair):
    size = pair.shape[0] // 2
    zero = jnp.zeros((size, pair.shape[1]), pair.dtype)
    return jnp.concatenate(
        [
            jnp.concatenate([pair[:size], zero], axis=1),
            jnp.concatenate([zero, pair[size:]], axis=1),
        ],
        axis=0,
    )


def head_rows(both):
    size, count = both.shape[0] // 2, both.shape[1] // 2
    return jnp.concatenate([both[:size, :count], both[size:, count:]], axis=0)


def twice(values):
    return jnp.concatenate([values, values], axis=1)


def fold(values):
    return values.reshape(values.shape[0] // 8, 8, values.shape[1])


class Mesh2:
    def __init__(self):
        self.row = lax.axis_index("dp")
        self.place = lax.axis_index("seq")
        self.side, self.core = self.place // 2, lax.rem(self.place, 2)
        self.sibling = self.side * 2 + 1 - self.core
        self.across = (1 - self.side) * 2 + self.core
        self.diagonal = (1 - self.side) * 2 + 1 - self.core
        self.core_peer = (self.row, self.sibling)
        self.y_peer = (self.row, self.across)

    def greet(self, peers):
        barrier = pltpu.get_barrier_semaphore()
        for peer in peers:
            pl.semaphore_signal(barrier, inc=1, device_id=peer, device_id_type=MESH)
        pl.semaphore_wait(barrier, len(peers))


def send(src, dst, sems, slot, peer):
    return pltpu.make_async_remote_copy(
        src_ref=src,
        dst_ref=dst,
        send_sem=sems.at[(0, *slot)],
        recv_sem=sems.at[(1, *slot)],
        device_id=peer,
        device_id_type=MESH,
    )


def softmax_pair(pair, r, count, steps, keys, turned, terms, queries_t, masses, out_t, probs, place):
    lanes = block(pair, 2 * r.head_dim)
    queries = head_blocks(queries_t[lanes, :])
    near = place is not None
    if near:
        tiles = [
            pltpu.roll(
                jnp.broadcast_to(r.near_bias[pl.ds(pair * 2 + head, 1), :], (NEAR, 2 * NEAR)),
                0,
                1,
                stride=1,
                stride_axis=0,
            )
            for head in range(2)
        ]
        below = [tile[:, NEAR:] for tile in tiles]
        on = [tile[:, :NEAR] for tile in tiles]
        none = jnp.zeros((NEAR, NEAR), F32)
        before = jnp.concatenate([below[0], none, below[1], none], axis=1)
        first = jnp.concatenate([on[0], below[0], on[1], below[1]], axis=1)
        second = jnp.concatenate([none, on[0], none, on[1]], axis=1)

    top = jnp.full((8, 2 * count), -jnp.inf, F32)
    for index in range(steps):
        rows = block(index, count)
        raw = dot(keys[index, :, lanes], queries) + twice(terms[rows, :])
        r.scores[rows, :] = raw
        if not near:
            top = jnp.maximum(top, jnp.max(fold(raw), axis=0))
    if near:
        rows = block(place, count)
        r.scores[rows, :] = r.scores[rows, :] + jnp.concatenate([first, second], axis=0)

        @pl.when(place > 0)
        def _():
            last = block(place * (count // NEAR) - 1, NEAR)
            r.scores[last, :] = r.scores[last, :] + before

        for index in range(steps):
            top = jnp.maximum(top, jnp.max(fold(r.scores[block(index, count), :]), axis=0))
    top = jnp.max(top, axis=0, keepdims=True)
    mass = jnp.zeros((8, 2 * count), F32)
    context = jnp.zeros((2 * r.head_dim, 2 * count), F32)
    for index in range(steps):
        rows = block(index, count)
        weights = jnp.exp(r.scores[rows, :] - top)
        low = weights.astype(LOW)
        probs[rows, :] = low
        context = context + dot(turned[lanes, rows], low)
        mass = mass + jnp.sum(fold(weights), axis=0)
    inverse = 1.0 / jnp.sum(mass, axis=0, keepdims=True)
    masses[pair] = inverse
    out_t[lanes, :] = head_rows(context * inverse)


def forward_kernel(names, dims, *refs):
    r = SimpleNamespace(**dict(zip(names, refs)), head_dim=dims.head_dim)
    m = Mesh2()
    count, places, pairs, fan, width = dims.count, dims.places, dims.pairs, dims.fan, dims.width
    q_place = m.place

    def load(slot, src, dst):
        copy = pltpu.make_async_copy(src, dst, r.load_sem.at[slot])
        copy.start()
        return copy

    loads = SimpleNamespace(
        wk=load(0, r.wk_hbm, r.wk),
        wv=load(1, r.wv_hbm, r.wv),
        wq=load(2, r.wq_hbm, r.wq),
        wout=load(3, r.wout_hbm, r.wout),
        cwk=load(4, r.cwk_hbm, r.cwk),
        cwv=load(5, r.cwv_hbm, r.cwv),
        wo=load(6, r.wo_hbm, r.wo),
        cwq=load(7, r.cwq_hbm, r.cwq),
        cwo=load(8, r.cwo_hbm, r.cwo),
    )

    m.greet([m.core_peer, m.y_peer])
    x_y = send(r.x, r.xs.at[m.place], r.link_sem, (0,), m.y_peer)
    x_core = send(r.x, r.xs.at[m.place], r.link_sem, (1,), m.core_peer)
    x_on = send(r.xs.at[m.across], r.xs.at[m.across], r.link_sem, (2,), m.core_peer)
    e_y = send(r.e, r.es.at[m.place], r.link_sem, (3,), m.y_peer)
    e_core = send(r.e, r.es.at[m.place], r.link_sem, (4,), m.core_peer)
    e_on = send(r.es.at[m.across], r.es.at[m.across], r.link_sem, (5,), m.core_peer)
    x_y.start()
    x_core.start()
    e_core.start()
    r.xs[m.place] = r.x[...]
    r.es[m.place] = r.e[...]

    gain_self = r.gain_self[...].astype(F32).reshape(1, width)
    gain_cross = r.gain_cross[...].astype(F32).reshape(1, width)

    items = dims.items
    dec_starts, enc_starts = [0], [0]
    for index in range(items):
        dec_starts.append(dec_starts[-1] + r.dec_len[0, index])
        enc_starts.append(enc_starts[-1] + r.enc_len[0, index])
    query_at = q_place * count + lax.broadcasted_iota(jnp.int32, (1, count), 1)
    low_self = jnp.zeros((1, count), jnp.int32)
    low_cross = jnp.zeros((1, count), jnp.int32)
    high_cross = jnp.full((1, count), enc_starts[1], jnp.int32)
    for index in range(1, items):
        inside = query_at >= dec_starts[index]
        low_self = jnp.where(inside, dec_starts[index], low_self)
        low_cross = jnp.where(inside, enc_starts[index], low_cross)
        high_cross = jnp.where(inside, enc_starts[index + 1], high_cross)

    def masks(index, carry):
        rows = block(index, count)
        key_at = index * count + lax.broadcasted_iota(jnp.int32, (count, count), 0)
        r.self_terms[rows, :] = jnp.where((key_at >= low_self) & (key_at <= query_at), 0.0, NEG)
        r.cross_terms[rows, :] = jnp.where((key_at >= low_cross) & (key_at < high_cross), 0.0, NEG)
        return carry

    lax.fori_loop(0, places, masks, 0)

    buckets = r.table.shape[1]
    terms = bucket_terms(buckets)
    last = lax.broadcasted_iota(jnp.int32, terms.shape, 0) == buckets - 1
    terms = terms - last.astype(F32)
    r.near_bias[...] = dot(r.table[...], terms.astype(LOW))

    def self_block(place):
        rows = block(place, count)
        states = r.xs[place].astype(F32)
        normed = (states * scale_of(states) * gain_self).astype(LOW)
        r.a1[place] = normed
        r.keys[place] = dot(normed, r.wk[...]).astype(LOW)
        values = dot(normed, r.wv[...]).astype(LOW)
        r.values[place] = values
        r.values_t[:, rows] = jnp.transpose(values)

    def cross_block(place):
        rows = block(place, count)
        encoded = r.es[place]
        r.ckeys[place] = dot(encoded, r.cwk[...]).astype(LOW)
        values = dot(encoded, r.cwv[...]).astype(LOW)
        r.cvalues[place] = values
        r.cvalues_t[:, rows] = jnp.transpose(values)

    def nth_place(k):
        return lax.rem(m.side + k // 2, 2) * 2 + lax.rem(m.core + lax.rem(k, 2), 2)

    def cross_blocks(k, carry):
        @pl.when(k == 1)
        def _():
            e_core.wait()

        @pl.when(k == 3)
        def _():
            e_on.wait()

        cross_block(nth_place(k))
        return carry

    def inner_grad(index, carry):
        r.inner_grad[index] = dot_nt(r.go[...], r.wout[block(index, width), :]).astype(LOW)
        return carry

    def self_blocks(k, carry):
        @pl.when(k == 1)
        def _():
            x_core.wait()

        @pl.when(k == 2)
        def _():
            loads.wout.wait()
            lax.fori_loop(0, fan, inner_grad, 0)
            loads.cwk.wait()
            loads.cwv.wait()
            lax.fori_loop(0, 2, cross_blocks, 0)
            x_y.wait()
            x_on.start()
            e_y.start()

        @pl.when(k == 3)
        def _():
            x_on.wait()

        self_block(nth_place(k))

        @pl.when(k == 0)
        def _():
            loads.wq.wait()
            r.queries_t[...] = jnp.transpose(dot(r.a1[m.place], r.wq[...]).astype(LOW))

        return carry

    loads.wk.wait()
    loads.wv.wait()
    lax.fori_loop(0, 4, self_blocks, 0)

    def keep(src, dst, slot):
        copy = pltpu.make_async_copy(src, dst, r.keep_sem.at[slot])
        copy.start()
        return copy

    kept = [
        keep(r.keys, r.keys_out, 0),
        keep(r.values, r.values_out, 1),
        keep(r.a1, r.a1_out, 2),
        keep(r.inner_grad, r.inner_out, 6),
    ]

    def probs_copy(slot, out, pair):
        return pltpu.make_async_copy(r.probs.at[slot], out.at[pair], r.probs_sem.at[slot])

    def attend(earlier, keys, turned, terms, queries_t, masses, out_t, out, place):
        def one(pair, carry):
            slot = lax.rem(pair, 2)
            if earlier:
                probs_copy(slot, out, pair).wait()
            else:
                @pl.when(pair >= 2)
                def _():
                    probs_copy(slot, out, pair).wait()

                @pl.when(pair == pairs - 2)
                def _():
                    e_y.wait()
                    e_on.start()
            softmax_pair(
                pair, r, count, places, keys, turned, terms, queries_t, masses, out_t,
                r.probs.at[slot], place,
            )
            probs_copy(slot, out, pair).start()
            return carry

        lax.fori_loop(0, pairs, one, 0)

    attend(
        False, r.keys, r.values_t, r.self_terms, r.queries_t, r.self_masses, r.context_t,
        r.self_probs, q_place,
    )
    loads.wo.wait()
    context = jnp.transpose(r.context_t[...]).astype(LOW)
    first = r.x[...].astype(F32) + dot(context, r.wo[...])
    r.first[...] = first
    normed_cross = (first * scale_of(first) * gain_cross).astype(LOW)
    r.a2[...] = normed_cross
    loads.cwq.wait()
    r.cqueries_t[...] = jnp.transpose(dot(normed_cross, r.cwq[...]).astype(LOW))
    lax.fori_loop(2, 4, cross_blocks, 0)
    kept += [
        keep(r.ckeys, r.ckeys_out, 3),
        keep(r.cvalues, r.cvalues_out, 4),
        keep(r.es, r.es_out, 5),
    ]
    attend(
        True, r.ckeys, r.cvalues_t, r.cross_terms, r.cqueries_t, r.cross_masses, r.ccontext_t,
        r.cross_probs, None,
    )
    loads.cwo.wait()
    context = jnp.transpose(r.ccontext_t[...]).astype(LOW)
    r.second[...] = r.first[...] + dot(context, r.cwo[...])
    for slot in range(2):
        probs_copy(slot, r.cross_probs, pairs - 2 + slot).wait()
    for copy in kept:
        copy.wait()


def call(kernel, name, collective, limit, inputs, outputs, scratch, aliases=None):
    names = (*inputs, *outputs, *scratch)
    results = pl.pallas_call(
        functools.partial(kernel, names),
        out_shape=tuple(jax.ShapeDtypeStruct(shape, kind) for shape, kind, _ in outputs.values()),
        in_specs=[pl.BlockSpec(memory_space=space) for _, space in inputs.values()],
        out_specs=tuple(pl.BlockSpec(memory_space=space) for _, _, space in outputs.values()),
        scratch_shapes=list(scratch.values()),
        input_output_aliases=aliases or {},
        compiler_params=pltpu.CompilerParams(
            collective_id=collective, has_side_effects=True, vmem_limit_bytes=limit * 2**20
        ),
        name=name,
    )(*(array for array, _ in inputs.values()))
    return SimpleNamespace(**dict(zip(outputs, results)))


def run_forward(dims, a):
    count, total, width = dims.count, dims.count * dims.places, dims.width
    near, far, scalars = pltpu.VMEM, pl.ANY, pltpu.SMEM
    pairs, fan = dims.pairs, dims.fan
    square = (width, width)
    own = (count, width)
    inputs = dict(
        x=(a.dec_states[0], near),
        e=(a.enc_states[0], near),
        go=(a.out_grad[0], near),
        dec_len=(a.dec_lengths, scalars),
        enc_len=(a.enc_lengths, scalars),
        table=(a.position_bias.T, near),
        gain_self=(a.gain_self, near),
        gain_cross=(a.gain_cross, near),
        wk_hbm=(a.self_key, far),
        wv_hbm=(a.self_value, far),
        wq_hbm=(a.self_query, far),
        wout_hbm=(a.ffn_out, far),
        cwk_hbm=(a.cross_key, far),
        cwv_hbm=(a.cross_value, far),
        wo_hbm=(a.self_output, far),
        cwq_hbm=(a.cross_query, far),
        cwo_hbm=(a.cross_output, far),
    )
    outputs = dict(
        first=(own, F32, near),
        second=(own, F32, near),
        inner_out=((fan, *own), LOW, far),
        queries_t=((width, count), LOW, near),
        cqueries_t=((width, count), LOW, near),
        context_t=((width, count), F32, near),
        ccontext_t=((width, count), F32, near),
        self_masses=((pairs, 1, 2 * count), F32, near),
        cross_masses=((pairs, 1, 2 * count), F32, near),
        a2=(own, LOW, near),
        keys_out=((dims.places, *own), LOW, far),
        values_out=((dims.places, *own), LOW, far),
        a1_out=((dims.places, *own), LOW, far),
        ckeys_out=((dims.places, *own), LOW, far),
        cvalues_out=((dims.places, *own), LOW, far),
        es_out=((dims.places, *own), LOW, far),
        self_probs=((pairs, total, 2 * count), LOW, far),
        cross_probs=((pairs, total, 2 * count), LOW, far),
    )
    scratch = dict(
        xs=pltpu.VMEM((dims.places, *own), LOW),
        es=pltpu.VMEM((dims.places, *own), LOW),
        wk=pltpu.VMEM(square, LOW),
        wv=pltpu.VMEM(square, LOW),
        wq=pltpu.VMEM(square, LOW),
        wout=pltpu.VMEM((fan * width, width), LOW),
        cwk=pltpu.VMEM(square, LOW),
        cwv=pltpu.VMEM(square, LOW),
        wo=pltpu.VMEM(square, LOW),
        cwq=pltpu.VMEM(square, LOW),
        cwo=pltpu.VMEM(square, LOW),
        a1=pltpu.VMEM((dims.places, *own), LOW),
        keys=pltpu.VMEM((dims.places, *own), LOW),
        values=pltpu.VMEM((dims.places, *own), LOW),
        values_t=pltpu.VMEM((width, total), LOW),
        ckeys=pltpu.VMEM((dims.places, *own), LOW),
        cvalues=pltpu.VMEM((dims.places, *own), LOW),
        cvalues_t=pltpu.VMEM((width, total), LOW),
        self_terms=pltpu.VMEM((total, count), F32),
        cross_terms=pltpu.VMEM((total, count), F32),
        near_bias=pltpu.VMEM((dims.heads, 2 * NEAR), F32),
        scores=pltpu.VMEM((total, 2 * count), F32),
        probs=pltpu.VMEM((2, total, 2 * count), LOW),
        inner_grad=pltpu.VMEM((fan, *own), LOW),
        load_sem=pltpu.SemaphoreType.DMA((10,)),
        link_sem=pltpu.SemaphoreType.DMA((2, 6)),
        keep_sem=pltpu.SemaphoreType.DMA((7,)),
        probs_sem=pltpu.SemaphoreType.DMA((2,)),
    )
    return call(
        lambda names, *refs: forward_kernel(names, dims, *refs),
        "forward", 0, 56, inputs, outputs, scratch,
    )


SWAPPED = (1, 4, 6, 8, 10, 13, 16, 19, 22)


class Reducer:
    LAGS = (0, 3, 5, 7, 10, 14)

    def __init__(self, r, m, dims):
        self.r, self.m = r, m
        self.planes = dims.planes
        self.line = dims.line
        self.piece = dims.piece
        self.chunk_rows = dims.chunk_rows
        self.half_rows = dims.chunk_rows // 2
        self.chunks = dims.chunks
        self.ring = dims.ring
        self.plane, self.half = m.row // 2, lax.rem(m.row, 2)
        self.x_peer = (self.plane * 2 + 1 - self.half, m.place)
        self.published = self.loaded = self.fed = self.moved = 0

    def z_peer(self, step):
        return (lax.rem(self.plane + step, self.planes) * 2 + self.half, self.m.place)

    def plane_peer(self, plane):
        return (plane * 2 + self.half, self.m.place)

    def peers(self):
        return [self.x_peer] + [self.z_peer(step) for step in range(1, self.planes)]

    def span(self, first, size):
        return pl.ds(pl.multiple_of(first, self.piece), size)

    def rows(self, index):
        return self.span(index * self.chunk_rows, self.chunk_rows)

    def by_planes(self, index):
        found = index == SWAPPED[0]
        for other in SWAPPED[1:]:
            found = found | (index == other)
        return found

    def route(self, index, first, other):
        if not self.line:
            first(index)
            return
        special = self.by_planes(index)

        @pl.when(jnp.logical_not(special))
        def _():
            first(index)

        @pl.when(special)
        def _():
            other(index)

    def half_of(self, index, half):
        return self.span(index * self.chunk_rows + half * self.half_rows, self.half_rows)

    def packed(self, index):
        return self.span(index * self.half_rows, self.half_rows)

    def fresh_rows(self, index):
        return self.span(lax.rem(index, self.ring) * self.chunk_rows, self.chunk_rows)

    def load(self, index):
        r = self.r
        return pltpu.make_async_copy(
            r.big.at[self.m.core, :, self.rows(index)],
            r.fresh.at[:, self.fresh_rows(index)],
            r.chunk_sem.at[index],
        )

    def core_copy(self, index):
        r, rows = self.r, self.rows(index)
        return send(
            r.big.at[1 - self.m.core, :, rows], r.sums.at[:, rows], r.core_sem, (index,),
            self.m.core_peer,
        )

    def y_copy(self, index):
        r, rows = self.r, self.rows(index)
        return send(
            r.sums.at[1 - self.m.side, rows], r.fin.at[rows], r.y_sem, (index,), self.m.y_peer
        )

    def x_copy(self, index):
        r = self.r
        return send(
            r.sums.at[self.m.side, self.half_of(index, 1 - self.half)],
            r.x_recv.at[self.packed(index)],
            r.x_sem, (index,), self.x_peer,
        )

    def in_copy(self, index, inner):
        r = self.r
        return send(
            r.sums.at[self.m.side, self.half_of(index, self.half)],
            r.z_recv.at[0, self.packed(index)],
            r.z_sem, (index, 0), self.plane_peer(inner),
        )

    def mid_copy(self, index):
        r = self.r
        return send(
            r.sums.at[self.m.side, self.half_of(index, self.half)],
            r.z_recv.at[1, self.packed(index)],
            r.z_sem, (index, 1), self.plane_peer(3 - self.plane),
        )

    def out_copy(self, index, outer):
        r, rows = self.r, self.half_of(index, self.half)
        return send(r.fin.at[rows], r.fin.at[rows], r.gz_sem, (index, 0), self.plane_peer(outer))

    def z_part(self, index, which):
        first = index * self.chunk_rows + self.half * self.half_rows + which * self.piece
        return self.span(first, self.piece)

    def z_copy(self, index, step):
        r = self.r
        target = lax.rem(self.plane + step, self.planes)
        return send(
            r.sums.at[self.m.side, self.z_part(index, target)],
            r.z_recv.at[step - 1, self.span(index * self.piece, self.piece)],
            r.z_sem, (index, step - 1), self.z_peer(step),
        )

    def gz_copy(self, index, step):
        r, rows = self.r, self.z_part(index, self.plane)
        return send(r.fin.at[rows], r.fin.at[rows], r.gz_sem, (index, step - 1), self.z_peer(step))

    def gx_copy(self, index):
        r, rows = self.r, self.half_of(index, self.half)
        return send(r.fin.at[rows], r.fin.at[rows], r.gx_sem, (index,), self.x_peer)

    def publish(self, rows):
        last = rows // self.chunk_rows

        def begin(index, carry):
            self.core_copy(index).start()
            return carry

        def fetch(index, carry):
            self.load(index).start()
            return carry

        lax.fori_loop(self.published, last, begin, 0)
        ahead = min(last, self.fed + self.ring)
        lax.fori_loop(self.loaded, ahead, fetch, 0)
        self.published, self.loaded = last, max(self.loaded, ahead)

    def publish_part(self, first, last):
        def begin(index, carry):
            self.core_copy(index).start()

            @pl.when(index < self.ring)
            def _():
                self.load(index).start()

            return carry

        lax.fori_loop(first, last, begin, 0)

    def parts_done(self, last, fed):
        self.published, self.fed = last, fed
        self.loaded = min(last, self.ring)

    def feed(self, index, prefetch=True):
        r = self.r
        self.load(index).wait()
        self.core_copy(index).wait()
        rows, fresh = self.rows(index), self.fresh_rows(index)
        for side in range(2):
            r.sums[side, rows, :] = add_low(r.sums[side, rows, :], r.fresh[side, fresh, :])
        self.route(
            index, lambda at: self.y_copy(at).start(), lambda at: self.swap_copy(at).start()
        )

        if not prefetch:
            return

        @pl.when(index + self.ring < self.published)
        def _():
            self.load(index + self.ring).start()

    def move(self, step):
        stages = (
            (self.after_y, self.after_swap),
            (self.after_x, self.swapped_y),
            (self.inward, self.swapped_x),
            (self.middle, self.swapped_pair),
            (self.outward, self.swapped_back),
            (self.finish, self.swapped_finish),
        )
        for lag, stage in reversed(tuple(zip(self.LAGS, stages))):
            index = step - lag

            @pl.when((index >= 0) & (index < self.chunks))
            def _():
                self.route(index, *stage)


    def parity(self):
        return lax.rem(self.plane, 2)

    def neighbour(self):
        return self.plane_peer(self.plane + 1 - 2 * self.parity())

    def quarter_of(self, index, half):
        size = self.half_rows // 2
        first = index * self.chunk_rows + self.parity() * self.half_rows + half * size
        return self.span(first, size)

    def packed_quarter(self, index, which):
        size = self.half_rows // 2
        return self.span(index * self.half_rows + which * size, size)

    def swap_copy(self, index):
        r = self.r
        return send(
            r.sums.at[:, self.half_of(index, 1 - self.parity())],
            r.z_recv.at[:, self.packed(index)],
            r.z_sem, (index, 0), self.neighbour(),
        )

    def swapped_y_copy(self, index):
        r, rows = self.r, self.half_of(index, self.parity())
        return send(
            r.sums.at[1 - self.m.side, rows], r.fin.at[rows], r.y_sem, (index,), self.m.y_peer
        )

    def swapped_x_copy(self, index):
        r = self.r
        return send(
            r.sums.at[self.m.side, self.quarter_of(index, 1 - self.half)],
            r.x_recv.at[self.packed_quarter(index, 0)],
            r.x_sem, (index,), self.x_peer,
        )

    def pair_copy(self, index):
        r = self.r
        return send(
            r.sums.at[self.m.side, self.quarter_of(index, self.half)],
            r.x_recv.at[self.packed_quarter(index, 1)],
            r.z_sem, (index, 1), self.z_peer(2),
        )

    def swapped_gx_copy(self, index):
        r, rows = self.r, self.quarter_of(index, self.half)
        return send(r.fin.at[rows], r.fin.at[rows], r.gx_sem, (index,), self.x_peer)

    def swapped_gz_copy(self, index):
        r, rows = self.r, self.half_of(index, self.parity())
        return send(r.fin.at[rows], r.fin.at[rows], r.gz_sem, (index, 0), self.neighbour())

    def after_swap(self, index):
        r = self.r
        self.swap_copy(index).wait()
        rows, packed = self.half_of(index, self.parity()), self.packed(index)
        for side in range(2):
            r.sums[side, rows, :] = add_low(r.sums[side, rows, :], r.z_recv[side, packed, :])
        self.swapped_y_copy(index).start()

    def swapped_y(self, index):
        r, m = self.r, self.m
        self.swapped_y_copy(index).wait()
        rows = self.half_of(index, self.parity())
        r.sums[m.side, rows, :] = add_low(r.sums[m.side, rows, :], r.fin[rows, :])
        self.swapped_x_copy(index).start()

    def swapped_x(self, index):
        r, m = self.r, self.m
        self.swapped_x_copy(index).wait()
        rows = self.quarter_of(index, self.half)
        arrived = r.x_recv[self.packed_quarter(index, 0), :]
        r.sums[m.side, rows, :] = add_low(r.sums[m.side, rows, :], arrived)
        self.pair_copy(index).start()

    def swapped_pair(self, index):
        r, m = self.r, self.m
        self.pair_copy(index).wait()
        rows = self.quarter_of(index, self.half)
        arrived = r.x_recv[self.packed_quarter(index, 1), :]
        r.fin[rows, :] = add_low(r.sums[m.side, rows, :], arrived)
        self.swapped_gx_copy(index).start()

    def swapped_back(self, index):
        self.swapped_gx_copy(index).wait()
        self.swapped_gz_copy(index).start()

    def swapped_finish(self, index):
        self.swapped_gz_copy(index).wait()

    def after_y(self, index):
        r, m = self.r, self.m
        self.y_copy(index).wait()
        rows = self.rows(index)
        r.sums[m.side, rows, :] = add_low(r.sums[m.side, rows, :], r.fin[rows, :])
        self.x_copy(index).start()

    def after_x(self, index):
        r, m = self.r, self.m
        self.x_copy(index).wait()
        rows = self.half_of(index, self.half)
        r.sums[m.side, rows, :] = add_low(r.sums[m.side, rows, :], r.x_recv[self.packed(index), :])
        if not self.line:
            for step in range(1, self.planes):
                self.z_copy(index, step).start()
            return
        for outer, inner in ((0, 1), (3, 2)):
            @pl.when(self.plane == outer)
            def _():
                self.in_copy(index, inner).start()

    def inward(self, index):
        r, m = self.r, self.m
        if not self.line:
            return
        for outer, inner in ((0, 1), (3, 2)):
            @pl.when(self.plane == outer)
            def _():
                self.in_copy(index, inner).wait_send()

        @pl.when((self.plane == 1) | (self.plane == 2))
        def _():
            self.in_copy(index, self.plane).wait_recv()
            rows = self.half_of(index, self.half)
            arrived = r.z_recv[0, self.packed(index), :]
            r.sums[m.side, rows, :] = add_low(r.sums[m.side, rows, :], arrived)
            self.mid_copy(index).start()

    def middle(self, index):
        r, m = self.r, self.m
        if not self.line:
            part = self.z_part(index, self.plane)
            total = r.sums[m.side, part, :].astype(F32)
            for step in range(1, self.planes):
                self.z_copy(index, step).wait()
                arrived = r.z_recv[step - 1, self.span(index * self.piece, self.piece), :]
                total = total + arrived.astype(F32)
            r.fin[part, :] = total.astype(LOW)
            for step in range(1, self.planes):
                self.gz_copy(index, step).start()
            return

        @pl.when((self.plane == 1) | (self.plane == 2))
        def _():
            self.mid_copy(index).wait()
            rows = self.half_of(index, self.half)
            arrived = r.z_recv[1, self.packed(index), :]
            r.fin[rows, :] = add_low(r.sums[m.side, rows, :], arrived)
            for outer, inner in ((0, 1), (3, 2)):
                @pl.when(self.plane == inner)
                def _():
                    self.out_copy(index, outer).start()
            self.gx_copy(index).start()

    def outward(self, index):
        if not self.line:
            for step in range(1, self.planes):
                self.gz_copy(index, step).wait()
            self.gx_copy(index).start()
            return
        for outer, inner in ((0, 1), (3, 2)):
            @pl.when(self.plane == inner)
            def _():
                self.out_copy(index, outer).wait_send()

            @pl.when(self.plane == outer)
            def _():
                self.out_copy(index, inner).wait_recv()
                self.gx_copy(index).start()

    def finish(self, index):
        self.gx_copy(index).wait()

    def run(self, feeds, moves):
        loops = max(1, feeds, moves)
        one, after = self.beside(loops, feeds, moves)

        def body(index, carry):
            one(index)
            return carry

        lax.fori_loop(0, loops, body, 0)
        after()

    def beside(self, loops, feeds, moves):
        feeds = max(0, min(feeds, self.published - self.fed))
        fed = self.fed + feeds
        limit = self.chunks + self.LAGS[-1] if fed == self.chunks else fed
        moves = max(0, min(moves, limit - self.moved))
        first_feed, first_move = self.fed, self.moved

        each = -(-feeds // loops)

        def one(index):
            if feeds > 0:
                def feed(step, carry):
                    self.feed(first_feed + step)
                    return carry

                lax.fori_loop(
                    jnp.minimum(index * each, feeds), jnp.minimum((index + 1) * each, feeds), feed, 0
                )
            if moves > 0:
                def move(step, carry):
                    self.move(first_move + step)
                    return carry

                lax.fori_loop(index * moves // loops, (index + 1) * moves // loops, move, 0)

        def after():
            self.fed, self.moved = fed, first_move + moves
            self.loaded = max(self.loaded, min(self.published, self.fed + self.ring))

        return one, after

    def finish_all(self, each, events):
        feeds, moves = self.chunks - self.fed, self.left()
        first_feed, first_move = self.fed, self.moved
        events = [(min(step, moves - 1), event) for step, event in events]

        def body(step, carry):
            for at, event in events:
                @pl.when(step == at)
                def _():
                    event()

            def feed(index, carry):
                self.feed(first_feed + index)
                return carry

            lax.fori_loop(
                jnp.minimum(step * each, feeds), jnp.minimum((step + 1) * each, feeds), feed, 0
            )
            self.move(first_move + step)
            return carry

        lax.fori_loop(0, moves, body, 0)

    def left(self):
        return self.chunks + self.LAGS[-1] - self.moved


def attend_back(pair, r, count, keys, keys_t, values, queries_t, masses, context_t, grad_t, probs, place, places):
    lanes = block(pair, 2 * r.head_dim)
    inverse = masses[pair]
    grads = grad_t[lanes, :].astype(F32)
    product = grads * context_t[lanes, :]
    sums = [
        jnp.sum(product[: r.head_dim], axis=0, keepdims=True),
        jnp.sum(product[r.head_dim :], axis=0, keepdims=True),
    ]
    inner = jnp.concatenate(sums, axis=1) * inverse
    grads = (head_blocks(grads) * inverse).astype(LOW)
    queries = head_blocks(queries_t[lanes, :])

    total = jnp.zeros((2 * r.head_dim, 2 * count), F32)
    beyond = jnp.zeros((8, 2 * count), F32)
    split = count - NEAR
    if place is not None:
        r.before[...] = jnp.zeros_like(r.before)
    for index in range(places):
        rows = block(index, count)
        weights = probs[rows, :]
        score_grad = weights.astype(F32) * (dot(values[index, :, lanes], grads) - inner)
        low = score_grad.astype(LOW)
        r.value_grad[index, :, lanes] = dot_nt(weights, grads).astype(LOW)
        r.key_grad[index, :, lanes] = dot_nt(low, queries).astype(LOW)
        total = total + dot(keys_t[lanes, rows], low)
        if place is not None:
            early = jnp.sum(fold(score_grad[:split]), axis=0)
            late = jnp.sum(fold(score_grad[split:]), axis=0)
            beyond = beyond + jnp.where(index < place, early, 0.0)
            beyond = beyond + jnp.where(index < place - 1, late, 0.0)

            @pl.when(index == place - 1)
            def _():
                r.before[...] = score_grad[split:]

            @pl.when(index == place)
            def _():
                r.own[...] = score_grad

    if place is not None:
        own, before = r.own[...], r.before[...]
        parts = []
        for head in range(2):
            at = head * count
            on = own[:NEAR, at : at + NEAR] + own[NEAR:, at + NEAR : at + 2 * NEAR]
            below = before[:, at : at + NEAR] + own[:NEAR, at + NEAR : at + 2 * NEAR]
            both = jnp.concatenate([on, below], axis=1)
            summed = both[:8]
            for group in range(1, NEAR // 8):
                summed = summed + pltpu.roll(
                    both[8 * group : 8 * group + 8], 2 * NEAR - 8 * group, 1
                )
            parts.append(summed)
        summed = jnp.concatenate(parts, axis=0)
        sublane = lax.broadcasted_iota(jnp.int32, summed.shape, 0)
        for bit in (1, 2, 4):
            summed = jnp.where(
                (sublane & bit) != 0, pltpu.roll(summed, 2 * NEAR - bit, 1), summed
            )
        lane = lax.broadcasted_iota(jnp.int32, (1, 2 * NEAR), 1)
        for head in range(2):
            at = head * count
            line = jnp.sum(summed[8 * head : 8 * head + 8], axis=0, keepdims=True)
            rest = jnp.sum(beyond[:, at : at + count]) + jnp.sum(before[:, at + NEAR : at + 2 * NEAR])
            line = line + jnp.where(lane == 2 * NEAR - 1, rest, 0.0)
            r.by_distance[pl.ds(pair * 2 + head, 1), :] = line
    r.query_grad_t[lanes, :] = head_rows(total).astype(LOW)


FFN_FEEDS = 3
PLAN = (
    (0, 0), (0, 0), (3, 1), (2, 1), (0, 2), (1, 0),
    (0, 3), (3, 2), (27, 6), (3, 0), (19, 1),
)
TAIL_FEEDS = 1
TAIL = (3, 6, 15, 19, 31)


def backward_kernel(names, dims, *refs):
    r = SimpleNamespace(**dict(zip(names, refs)), head_dim=dims.head_dim)
    m = Mesh2()
    count, places, pairs, fan, width = dims.count, dims.places, dims.pairs, dims.fan, dims.width
    own = width // places
    engine = Reducer(r, m, dims)
    plan = iter(PLAN)
    r.wo, r.wq, r.wk, r.wv = (r.squares.at[index] for index in range(4))
    r.keys, r.values, r.key_grad, r.value_grad = (r.tall.at[pl.ds(4 * k, 4)] for k in range(4))

    loads = SimpleNamespace()
    slots = iter(range(r.load_sem.shape[0]))

    def later(src, dst):
        return pltpu.make_async_copy(src, dst, r.load_sem.at[next(slots)])

    def load(src, dst):
        copy = later(src, dst)
        copy.start()
        return copy

    def probs_copy(src, pair):
        slot = lax.rem(pair, 2)
        return pltpu.make_async_copy(src.at[pair], r.probs.at[slot], r.probs_sem.at[slot])

    third = width // count
    loads.second = load(r.second_hbm, r.second)

    def ffn_copies(index):
        rows = pl.ds(index * third, third)
        win = r.win_hbm.at[:, block(index, width)]
        return (
            pltpu.make_async_copy(win, r.squares.at[index], r.win_sem.at[index]),
            pltpu.make_async_copy(r.wout_hbm.at[rows], r.tall.at[rows], r.wout_sem.at[index]),
        )

    for index in range(fan):
        win, wout = ffn_copies(index)
        win.start()
        if index == 0:
            loads.inner = load(r.inner_hbm, r.value_grad)
        wout.start()
    probs_copy(r.cross_probs, 0).start()
    probs_copy(r.cross_probs, 1).start()
    loads.es0 = load(r.es_hbm.at[m.core], r.group.at[0])
    loads.es1 = load(r.es_hbm.at[m.core + 2], r.group.at[1])
    loads.cqueries = load(r.cqueries_hbm, r.cqueries_t)
    loads.ccontext = load(r.ccontext_hbm, r.ccontext_t)
    loads.queries = load(r.queries_hbm, r.queries_t)
    loads.context = load(r.context_hbm, r.context_t)
    loads.a2 = load(r.a2_hbm, r.a2)

    m.greet([m.core_peer, m.y_peer] + engine.peers())

    gain_self = r.gain_self[...].astype(F32).reshape(1, width)
    gain_cross = r.gain_cross[...].astype(F32).reshape(1, width)
    staged = {}

    def unit_copy(unit):
        rows = pl.ds(2 * width + unit * own, own)
        return pltpu.make_async_copy(
            r.stage.at[unit % 2], r.big.at[:, :, rows], r.stage_sem.at[unit % 2]
        )

    def give(unit, left_t, right):
        if unit - 2 in staged:
            staged.pop(unit - 2).wait()

        for place in range(places):
            grad = dot(left_t[place * own : (place + 1) * own, :], right)
            r.stage[unit % 2, place % 2, place // 2] = grad.astype(LOW)
        staged[unit] = unit_copy(unit)
        staged[unit].start()

    def settle(rows):
        for unit in sorted(staged):
            staged.pop(unit).wait()
        engine.publish(rows)

    def turn(src, dst):
        def one(index, carry):
            rows = block(index, count)
            dst[:, rows] = jnp.transpose(src[index])
            return carry

        lax.fori_loop(0, places, one, 0)

    def attend(src, queries_t, masses, context_t, grad_t, place):
        beside, after = engine.beside(pairs, *next(plan))

        def one(pair, carry):
            probs_copy(src, pair).wait()
            attend_back(
                pair, r, count, r.keys, r.keys_t, r.values, queries_t, masses, context_t, grad_t,
                r.probs.at[lax.rem(pair, 2)], place, places,
            )

            @pl.when(pair + 2 < pairs)
            def _():
                probs_copy(src, pair + 2).start()

            beside(pair)
            return carry

        lax.fori_loop(0, pairs, one, 0)
        after()

    def exchange(slot):
        copies = []
        for side in range(2):
            theirs = side * 2 + 1 - m.core
            for part, (src, dst) in enumerate(
                ((r.key_grad, r.key_recv), (r.value_grad, r.value_recv))
            ):
                copies.append(
                    send(
                        src.at[theirs], dst.at[slot, side], r.swap_sem, (slot, side, part),
                        m.core_peer,
                    )
                )
                copies[-1].start()
        return copies

    def chip_sum(grad, arrived):
        parts = [add_low(grad[side * 2 + m.core], arrived[side]) for side in range(2)]
        return jnp.concatenate(parts, axis=0)

    def partial(slot, side):
        key_grad = add_low(r.key_grad[side * 2 + m.core], r.key_recv[slot, side])
        value_grad = add_low(r.value_grad[side * 2 + m.core], r.value_recv[slot, side])
        return dot_nt(key_grad, r.wk[...]) + dot_nt(value_grad, r.wv[...])

    gain_ffn = r.gain_ffn[...].astype(F32).reshape(1, width)
    loads.second.wait()
    second = r.second[...]
    normed_ffn = (second * scale_of(second) * gain_ffn).astype(LOW)
    r.grad_t[...] = jnp.transpose(normed_ffn)
    r.a3[...] = normed_ffn
    r.dec_grad[...] = jnp.zeros_like(second)
    r.enc_grad[...] = jnp.zeros_like(second)
    loads.cwo, loads.cwq = later(r.cwo_hbm, r.wo), later(r.cwq_hbm, r.wq)
    loads.cwk, loads.cwv = later(r.cwk_hbm, r.wk), later(r.cwv_hbm, r.wv)
    loads.ckeys, loads.cvalues = later(r.ckeys_hbm, r.keys), later(r.cvalues_hbm, r.values)
    freed = ((loads.cwo,), (loads.cwq, loads.ckeys), (loads.cwk, loads.cvalues), (loads.cwv,))
    loads.inner.wait()

    def head_copy(index):
        return pltpu.make_async_copy(
            r.keys_t.at[:, pl.ds(0, width)],
            r.big.at[lax.rem(index, 2), index // 2, pl.ds(width, width)],
            r.head_sem,
        )

    def feed_forward(index, carry):
        slot = lax.rem(index, 2)
        win, wout = ffn_copies(index)
        win.wait()
        pre = dot(r.a3[...], r.squares[index])
        half = 0.5 + 0.5 * lax.erf(pre * (0.5**0.5))
        inner = (pre * half).astype(LOW)
        slope = half + pre * jnp.exp(-0.5 * pre * pre) * ((2.0 * math.pi) ** -0.5)
        pre_grad = (slope * r.value_grad[index].astype(F32)).astype(LOW)

        def rows_of(place, carry):
            grad = dot(r.grad_t[block(place, own), :], pre_grad)
            r.stage[slot, lax.rem(place, 2), place // 2] = grad.astype(LOW)
            return carry

        lax.fori_loop(0, places, rows_of, 0)
        tail = pltpu.make_async_copy(
            r.stage.at[slot], r.big.at[:, :, block(index, own)], r.stage_sem.at[slot]
        )
        tail.start()
        wout.wait()
        rows = r.tall[pl.ds(index * third, third)].reshape(width, width)
        r.dec_grad[...] += dot(inner, rows)
        r.enc_grad[...] += dot_nt(pre_grad, r.squares[index])

        @pl.when(index > 0)
        def _():
            head_copy(index - 1).wait()

        r.keys_t[:, :width] = dot(jnp.transpose(inner), r.go[...]).astype(LOW)
        head_copy(index).start()
        for step, copies in enumerate(freed):
            @pl.when(index == step)
            def _():
                for copy in copies:
                    copy.start()
        tail.wait()
        chunk_rows = engine.chunk_rows
        engine.publish_part(index * own // chunk_rows, (index + 1) * own // chunk_rows)

        def feed(step, carry):
            engine.feed(step, prefetch=False)
            return carry

        lax.fori_loop(index * ffn_feeds // fan, (index + 1) * ffn_feeds // fan, feed, 0)
        return carry

    ffn_feeds = min(FFN_FEEDS, fan * own // engine.chunk_rows)
    lax.fori_loop(0, fan, feed_forward, 0)
    engine.parts_done(fan * own // engine.chunk_rows, ffn_feeds)
    r.layer_out[...] = (second + r.dec_grad[...]).astype(LOW)
    second_part, gain_ffn_grad = norm_back(second, gain_ffn, r.enc_grad[...])
    loads.first = load(r.first_hbm, r.enc_grad)
    r.dec_grad[...] = r.go[...].astype(F32) + second_part
    r.tiny[0] = jnp.zeros(r.tiny.shape[1:], F32)
    r.tiny[0, 2:3] = gain_ffn_grad
    head_copy(fan - 1).wait()
    engine.publish(2 * width)
    engine.run(*next(plan))

    head_grad = r.dec_grad[...].astype(LOW)
    loads.cwo.wait()
    r.grad_t[...] = dot_nt(r.wo[...], head_grad).astype(LOW)
    loads.wo = load(r.wo_hbm, r.wo)
    engine.run(*next(plan))
    loads.ccontext.wait()
    r.query_grad_t[...] = r.ccontext_t[...].astype(LOW)
    give(0, r.query_grad_t, head_grad)
    loads.ckeys.wait()
    turn(r.keys, r.keys_t)
    loads.cvalues.wait()
    loads.cqueries.wait()
    attend(r.cross_probs, r.cqueries_t, r.cross_masses, r.ccontext_t, r.grad_t, None)
    copies = exchange(0)
    loads.keys = load(r.keys_hbm, r.keys)
    loads.values = load(r.values_hbm, r.values)
    probs_copy(r.self_probs, 0).start()
    probs_copy(r.self_probs, 1).start()
    query_grad = jnp.transpose(r.query_grad_t[...])
    engine.run(*next(plan))
    loads.cwq.wait()
    normed_grad = dot_nt(query_grad, r.wq[...])
    loads.wq = load(r.wq_hbm, r.wq)
    loads.first.wait()
    first_part, gain_cross_grad = norm_back(r.enc_grad[...], gain_cross, normed_grad)
    r.dec_grad[...] += first_part
    r.tiny[0, 1:2] = gain_cross_grad
    loads.a2.wait()
    r.query_grad_t[...] = jnp.transpose(r.a2[...])
    give(1, r.query_grad_t, query_grad)
    engine.run(*next(plan))
    loads.es0.wait()
    loads.es1.wait()
    for side in range(2):
        r.group_t[:, side * count : (side + 1) * count] = jnp.transpose(r.group[side])
    loads.a10 = load(r.a1_hbm.at[m.core], r.group.at[0])
    loads.a11 = load(r.a1_hbm.at[m.core + 2], r.group.at[1])
    for copy in copies:
        copy.wait()
    key_grad = chip_sum(r.key_grad, r.key_recv.at[0])
    value_grad = chip_sum(r.value_grad, r.value_recv.at[0])
    loads.cwk.wait()
    loads.cwv.wait()
    r.partial_low[...] = partial(0, 1 - m.side).astype(LOW)
    enc_copy = send(r.partial_low, r.partial_recv.at[0], r.link_sem, (0,), m.y_peer)
    enc_copy.start()
    r.enc_grad[...] = partial(0, m.side)
    loads.wk = load(r.wk_hbm, r.wk)
    loads.wv = load(r.wv_hbm, r.wv)
    engine.run(*next(plan))
    give(2, r.group_t, key_grad)
    give(3, r.group_t, value_grad)
    settle(3 * width)
    engine.run(*next(plan))

    first_grad = r.dec_grad[...]
    head_grad = first_grad.astype(LOW)
    loads.wo.wait()
    r.grad_t[...] = dot_nt(r.wo[...], head_grad).astype(LOW)
    loads.context.wait()
    engine.run(*next(plan))
    r.query_grad_t[...] = r.context_t[...].astype(LOW)
    give(4, r.query_grad_t, head_grad)
    loads.keys.wait()
    turn(r.keys, r.keys_t)
    loads.values.wait()
    loads.queries.wait()

    r.by_distance[...] = jnp.zeros_like(r.by_distance)
    attend(r.self_probs, r.queries_t, r.self_masses, r.context_t, r.grad_t, m.place)
    copies = exchange(1)
    query_grad = jnp.transpose(r.query_grad_t[...])
    engine.run(*next(plan))
    loads.wq.wait()
    normed_grad = dot_nt(query_grad, r.wq[...])
    loads.a10.wait()
    loads.a11.wait()
    for side in range(2):
        r.group_t[:, side * count : (side + 1) * count] = jnp.transpose(r.group[side])
    give(5, r.group_t.at[:, block(m.side, count)], query_grad)
    engine.run(*next(plan))
    for copy in copies:
        copy.wait()
    key_grad = chip_sum(r.key_grad, r.key_recv.at[1])
    value_grad = chip_sum(r.value_grad, r.value_recv.at[1])
    loads.wk.wait()
    loads.wv.wait()
    enc_copy.wait()
    r.enc_grad[...] += r.partial_recv[0].astype(F32)
    r.partial_low[...] = partial(1, 1 - m.side).astype(LOW)
    dec_copy = send(r.partial_low, r.partial_recv.at[1], r.link_sem, (1,), m.y_peer)
    dec_copy.start()
    normed_grad = normed_grad + partial(1, m.side)
    give(6, r.group_t, key_grad)
    give(7, r.group_t, value_grad)
    settle(4 * width)
    r.second[...] = normed_grad

    def hop(slot):
        peer = (m.core_peer, m.y_peer, engine.x_peer)[slot]
        return send(r.tiny.at[slot], r.tiny_recv.at[slot], r.tiny_sem, (slot,), peer)

    def spread(step):
        return send(
            r.tiny.at[3], r.tiny_recv.at[2 + step], r.tiny_sem, (2 + step,), engine.z_peer(step)
        )

    def arrive(slot):
        hop(slot).wait()
        r.tiny[slot + 1] = r.tiny[slot] + r.tiny_recv[slot]
        if slot < 2:
            hop(slot + 1).start()
            return
        for step in range(1, dims.planes):
            spread(step).start()

    def states():
        dec_copy.wait()
        normed_grad = r.second[...] + r.partial_recv[1].astype(F32)
        state_part, gain_self_grad = norm_back(r.x[...].astype(F32), gain_self, normed_grad)
        r.dec_grad[...] += state_part
        buckets = dims.buckets
        table = lax.dot_general(
            bucket_terms(buckets), r.by_distance[...], (((1,), (1,)), ((), ())),
            precision=lax.Precision.HIGHEST, preferred_element_type=F32,
        )
        r.tiny[0, 0:1] = gain_self_grad
        part = buckets // places
        for place in range(places):
            r.tiny[0, 8 : 8 + part, 128 * place : 128 * (place + 1)] = table[
                place * part : (place + 1) * part
            ]
        hop(0).start()

    def totals():
        total = r.tiny[3]
        for step in range(1, dims.planes):
            spread(step).wait()
            total = total + r.tiny_recv[2 + step]
        r.small[...] = total

    steps = (states, lambda: arrive(0), lambda: arrive(1), lambda: arrive(2), totals)
    engine.finish_all(TAIL_FEEDS, tuple(zip(TAIL, steps)))


def run_backward(dims, a, f):
    count, total, width = dims.count, dims.count * dims.places, dims.width
    near, far = pltpu.VMEM, pl.ANY
    pairs, planes, chunks, piece = dims.pairs, dims.planes, dims.chunks, dims.piece
    square = (width, width)
    own = (count, width)
    inputs = dict(
        x=(a.dec_states[0], near),
        go=(a.out_grad[0], near),
        gain_self=(a.gain_self, near),
        gain_cross=(a.gain_cross, near),
        gain_ffn=(a.gain_ffn, near),
        self_masses=(f.self_masses, near),
        cross_masses=(f.cross_masses, near),
        first_hbm=(f.first, far),
        second_hbm=(f.second, far),
        inner_hbm=(f.inner_out, far),
        win_hbm=(a.ffn_in, far),
        wout_hbm=(a.ffn_out.reshape(-1, *own), far),
        queries_hbm=(f.queries_t, far),
        cqueries_hbm=(f.cqueries_t, far),
        context_hbm=(f.context_t, far),
        ccontext_hbm=(f.ccontext_t, far),
        a2_hbm=(f.a2, far),
        keys_hbm=(f.keys_out, far),
        values_hbm=(f.values_out, far),
        a1_hbm=(f.a1_out, far),
        ckeys_hbm=(f.ckeys_out, far),
        cvalues_hbm=(f.cvalues_out, far),
        es_hbm=(f.es_out, far),
        self_probs=(f.self_probs, far),
        cross_probs=(f.cross_probs, far),
        wo_hbm=(a.self_output, far),
        wq_hbm=(a.self_query, far),
        wk_hbm=(a.self_key, far),
        wv_hbm=(a.self_value, far),
        cwo_hbm=(a.cross_output, far),
        cwq_hbm=(a.cross_query, far),
        cwk_hbm=(a.cross_key, far),
        cwv_hbm=(a.cross_value, far),
    )
    outputs = dict(
        big=((2, 2, 4 * width, width), LOW, far),
        layer_out=(own, LOW, near),
        fin=((4 * width, width), LOW, near),
        dec_grad=(own, F32, near),
        enc_grad=(own, F32, near),
        small=((16, width), F32, near),
    )
    dma = pltpu.SemaphoreType.DMA
    rows = 4 * width
    scratch = dict(
        squares=pltpu.VMEM((4, *square), LOW),
        tall=pltpu.VMEM((16, *own), LOW),
        second=pltpu.VMEM(own, F32),
        keys_t=pltpu.VMEM((width, total), LOW),
        probs=pltpu.VMEM((2, total, 2 * count), LOW),
        grad_t=pltpu.VMEM((width, count), LOW),
        a3=pltpu.VMEM(own, LOW),
        a2=pltpu.VMEM(own, LOW),
        queries_t=pltpu.VMEM((width, count), LOW),
        cqueries_t=pltpu.VMEM((width, count), LOW),
        context_t=pltpu.VMEM((width, count), F32),
        ccontext_t=pltpu.VMEM((width, count), F32),
        query_grad_t=pltpu.VMEM((width, count), LOW),
        key_recv=pltpu.VMEM((2, 2, *own), LOW),
        value_recv=pltpu.VMEM((2, 2, *own), LOW),
        partial_low=pltpu.VMEM(own, LOW),
        partial_recv=pltpu.VMEM((2, *own), LOW),
        group=pltpu.VMEM((2, *own), LOW),
        group_t=pltpu.VMEM((width, 2 * count), LOW),
        before=pltpu.VMEM((NEAR, 2 * count), F32),
        own=pltpu.VMEM((count, 2 * count), F32),
        by_distance=pltpu.VMEM((128, 2 * NEAR), F32),
        stage=pltpu.VMEM((2, 2, 2, width // dims.places, width), LOW),
        fresh=pltpu.VMEM((2, dims.ring * dims.chunk_rows, width), LOW),
        sums=pltpu.VMEM((2, rows, width), LOW),
        x_recv=pltpu.VMEM((rows // 2, width), LOW),
        z_recv=pltpu.VMEM(
            (2, rows // 2, width) if dims.line else (planes - 1, chunks * piece, width), LOW
        ),
        tiny=pltpu.VMEM((4, 16, width), F32),
        tiny_recv=pltpu.VMEM((2 + planes, 16, width), F32),
        load_sem=dma((40,)),
        win_sem=dma((4,)),
        wout_sem=dma((4,)),
        head_sem=dma,
        probs_sem=dma((2,)),
        stage_sem=dma((2,)),
        link_sem=dma((2, 2)),
        swap_sem=dma((2, 2, 2, 2)),
        chunk_sem=dma((chunks,)),
        core_sem=dma((2, chunks)),
        y_sem=dma((2, chunks)),
        x_sem=dma((2, chunks)),
        z_sem=dma((2, chunks, planes - 1)),
        gz_sem=dma((2, chunks, planes - 1)),
        gx_sem=dma((2, chunks)),
        tiny_sem=dma((2, 2 + planes)),
    )
    return call(
        lambda names, *refs: backward_kernel(names, dims, *refs),
        "backward", 1, 63, inputs, outputs, scratch,
    )


def place_kernel(names, dims, *refs):
    r = SimpleNamespace(**dict(zip(names, refs)))
    width, fan = dims.width, dims.fan
    own = width // dims.places
    passed = (
        (r.layer_in, r.layer_held, r.layer),
        (r.dec_in, r.dec_held, r.dec),
        (r.enc_in, r.enc_held, r.enc),
    )
    inward = [
        pltpu.make_async_copy(src, held, r.pass_sem.at[0, slot])
        for slot, (src, held, _) in enumerate(passed)
    ]
    copies = [
        pltpu.make_async_copy(held, dst, r.pass_sem.at[1, slot])
        for slot, (_, held, dst) in enumerate(passed)
    ]
    groups = 4 * width // own
    loads, stores = [], []
    for index in range(4):
        rows = pl.ds(index * width, width)
        loads.append(pltpu.make_async_copy(r.fin.at[rows], r.low.at[rows], r.load_sem.at[index]))
        loads[-1].start()
    for copy in inward:
        copy.start()
    units = (
        r.cross_output, r.cross_query, r.cross_key, r.cross_value,
        r.self_output, r.self_query, r.self_key, r.self_value,
    )
    for index in range(groups):
        if index % (groups // 4) == 0:
            loads[index // (groups // 4)].wait()
        rows = pl.ds(index * own, own)
        r.wide[rows, :] = r.low[rows, :].astype(F32)
        if index < fan:
            dst = r.ffn_in.at[:, pl.ds(index * width, width)]
        elif index < 2 * fan:
            dst = r.ffn_out.at[pl.ds((index - fan) * own, own)]
        else:
            dst = units[index - 2 * fan]
        copy = pltpu.make_async_copy(r.wide.at[rows], dst, r.store_sem.at[index])
        copy.start()
        stores.append(copy)
    for arrival, copy in zip(inward, copies):
        arrival.wait()
        copy.start()
    at = lax.axis_index("seq")
    part = dims.buckets // dims.places
    for place in range(dims.places):
        @pl.when(at == place)
        def _():
            for index, grad in enumerate((r.gain_self, r.gain_cross, r.gain_ffn)):
                grad[...] = r.small[index : index + 1, place * own : (place + 1) * own]
            r.table_grad[...] = r.small[8 : 8 + part, 128 * place : 128 * place + dims.heads]
    for copy in stores + copies:
        copy.wait()


def run_place(dims, f, b):
    near, far = pltpu.VMEM, pl.ANY
    width, own = dims.width, dims.width // dims.places
    square, gain = ((own, width), F32, far), ((1, own), F32, near)
    rows = 4 * width
    inputs = dict(
        fin=(b.fin, far),
        small=(b.small, near),
        layer_in=(b.layer_out, far),
        dec_in=(b.dec_grad, far),
        enc_in=(b.enc_grad, far),
    )
    outputs = dict(
        layer=(b.layer_out.shape, LOW, far),
        dec=(b.dec_grad.shape, F32, far),
        enc=(b.enc_grad.shape, F32, far),
        ffn_out=((width, width), F32, far),
        ffn_in=((own, dims.fan * width), F32, far),
        cross_output=square,
        cross_query=square,
        cross_key=square,
        cross_value=square,
        self_output=square,
        self_query=square,
        self_key=square,
        self_value=square,
        gain_self=gain,
        gain_cross=gain,
        gain_ffn=gain,
        table_grad=((dims.buckets // dims.places, dims.heads), F32, near),
    )
    scratch = dict(
        low=pltpu.VMEM((rows, width), LOW),
        wide=pltpu.VMEM((rows, width), F32),
        layer_held=pltpu.VMEM(b.layer_out.shape, LOW),
        dec_held=pltpu.VMEM(b.dec_grad.shape, F32),
        enc_held=pltpu.VMEM(b.enc_grad.shape, F32),
        pass_sem=pltpu.SemaphoreType.DMA((2, 3)),
        load_sem=pltpu.SemaphoreType.DMA((4,)),
        store_sem=pltpu.SemaphoreType.DMA((rows // own,)),
    )
    names = (*inputs, *outputs, *scratch)
    results = pl.pallas_call(
        lambda *refs: place_kernel(names, dims, *refs),
        out_shape=tuple(jax.ShapeDtypeStruct(shape, kind) for shape, kind, _ in outputs.values()),
        in_specs=[pl.BlockSpec(memory_space=space) for _, space in inputs.values()],
        out_specs=tuple(pl.BlockSpec(memory_space=space) for _, _, space in outputs.values()),
        scratch_shapes=list(scratch.values()),
        compiler_params=pltpu.CompilerParams(vmem_limit_bytes=60 * 2**20),
        name="place",
    )(*(array for array, _ in inputs.values()))
    return SimpleNamespace(**dict(zip(outputs, results)))


def on_device(
    dec_states,
    enc_states,
    out_grad,
    dec_lengths,
    enc_lengths,
    self_query,
    self_key,
    self_value,
    self_output,
    cross_query,
    cross_key,
    cross_value,
    cross_output,
    ffn_in,
    ffn_out,
    gain_self,
    gain_cross,
    gain_ffn,
    position_bias,
):
    a = SimpleNamespace(
        dec_states=dec_states,
        enc_states=enc_states,
        out_grad=out_grad,
        dec_lengths=dec_lengths,
        enc_lengths=enc_lengths,
        self_query=self_query,
        self_key=self_key,
        self_value=self_value,
        self_output=self_output,
        cross_query=cross_query,
        cross_key=cross_key,
        cross_value=cross_value,
        cross_output=cross_output,
        ffn_in=ffn_in,
        ffn_out=ffn_out,
        gain_self=gain_self,
        gain_cross=gain_cross,
        gain_ffn=gain_ffn,
        position_bias=position_bias,
    )
    count, width = a.dec_states.shape[1:]
    buckets, heads = a.position_bias.shape
    planes, piece = lax.axis_size("dp") // 2, 16
    line = planes == 4
    chunk_rows = 128 if line else 2 * planes * piece
    chunks = 4 * width // chunk_rows
    dims = SimpleNamespace(
        count=count,
        width=width,
        places=lax.axis_size("seq"),
        heads=heads,
        head_dim=width // heads,
        pairs=heads // 2,
        fan=a.ffn_in.shape[1] // width,
        items=a.dec_lengths.shape[1],
        buckets=buckets,
        planes=planes,
        piece=piece,
        chunks=chunks,
        ring=4 if line else 1,
        line=line,
        chunk_rows=chunk_rows,
    )
    f = run_forward(dims, a)
    b = run_backward(dims, a, f)
    o = run_place(dims, f, b)
    return (
        o.layer[None],
        o.dec[None],
        o.enc[None],
        o.self_query,
        o.self_key,
        o.self_value,
        o.self_output,
        o.cross_query,
        o.cross_key,
        o.cross_value,
        o.cross_output,
        o.ffn_in,
        o.ffn_out,
        o.gain_self[0],
        o.gain_cross[0],
        o.gain_ffn[0],
        o.table_grad,
    )


def solution(mesh):
    split = P("dp", "seq", None)
    rows = P("seq", None)
    return jax.shard_map(
        on_device,
        mesh=mesh,
        in_specs=(split,) * 3 + (P("dp", None),) * 2 + (P(),) * 14,
        out_specs=(split,) * 3 + (rows,) * 10 + (P("seq"),) * 3 + (rows,),
        check_vma=False,
    )
```

profile of v0, /device:TPU:0, one launch (start us, length us, event | category | flops | bytes accessed | tf_op | source)
XLA Modules:
  0.0 193.8 jit_solution(9252328139685907759)
XLA Ops:
  0.7 38.1 %forward.1 = (f32[256,768]{1,0:T(8,128)}, f32[256,768]{1,0:T(8,128)}, bf16[4,256,768]{2,1,0:T(8,128)(2,1)}, bf16[768,256]{1,0:T(8,128)(2,1)}, bf16[768,256]{1,0:...) custom-call(bf16[256,768]{1,0:T(8,128)(2,1)} %bitcast.12, ...), custom_call_target="tpu_custom_call" | custom-call | tf_op jit(solution)/shard_map/forward/pallas_call | solution.py:379
  38.8 147.4 %backward.1 = (bf16[2,2,3072,768]{3,2,1,0:T(8,128)(2,1)}, bf16[256,768]{1,0:T(8,128)(2,1)}, bf16[3072,768]{1,0:T(8,128)(2,1)}, f32[256,768]{1,0:T(8,128)}, f32[256,768]{1,0:T(8,128)}, /*index=5*/f32[16,768]{1,0:T(8,128)}) custom-call(bf16[256,768]{1,0:T(8,128)(2,1)} %bitcast.13, bf16[256,768]{1,0:T(8,128)(2,1)} %bitcast.15, bf16[768]{0:T(1024)(128)(2,1)} %refs_2_.1, ...), custom_call_target="tpu_custom_call" | custom-call | tf_op jit(solution)/shard_map/backward/pallas_call | solution.py:379
  186.2 7.4 %place.1 = (bf16[256,768]{1,0:T(8,128)(2,1)}, f32[256,768]{1,0:T(8,128)}, f32[256,768]{1,0:T(8,128)}, f32[768,768]{1,0:T(8,128)}, f32[192,3072]{1,0:T(8,128)}, /...) custom-call(bf16[3072,768]{1,0:T(8,128)(2,1)} %get-tuple-element.75., ...), custom_call_target="tpu_custom_call" | custom-call | tf_op jit(solution)/shard_map/place/pallas_call | solution.py:1561
where the time goes:
time: 194 us
  Pallas kernels  193 us (99%)
    pallas_call x2, Pallas kernels, call(): pl.pallas_call(functools.partial(kernel, names), out_shape=tuple((jax.Sha...  186 us
    pallas_call x1, Pallas kernels, run_place(): pl.pallas_call(lambda *refs: place_kernel(names, dims, *refs), out_shape=...  7.41 us

commit v1 on v0

--- a/solution.py
+++ b/solution.py
@@ -178,6 +178,9 @@
         return copy
 
     loads = SimpleNamespace(
+        x=load(9, r.x_hbm, r.xs.at[m.place]),
+        e=load(10, r.e_hbm, r.es.at[m.place]),
+        go=load(11, r.go_hbm, r.go),
         wk=load(0, r.wk_hbm, r.wk),
         wv=load(1, r.wv_hbm, r.wv),
         wq=load(2, r.wq_hbm, r.wq),
@@ -190,17 +193,15 @@
     )
 
     m.greet([m.core_peer, m.y_peer])
-    x_y = send(r.x, r.xs.at[m.place], r.link_sem, (0,), m.y_peer)
-    x_core = send(r.x, r.xs.at[m.place], r.link_sem, (1,), m.core_peer)
+    x_y = send(r.x_hbm, r.xs.at[m.place], r.link_sem, (0,), m.y_peer)
+    x_core = send(r.x_hbm, r.xs.at[m.place], r.link_sem, (1,), m.core_peer)
     x_on = send(r.xs.at[m.across], r.xs.at[m.across], r.link_sem, (2,), m.core_peer)
-    e_y = send(r.e, r.es.at[m.place], r.link_sem, (3,), m.y_peer)
-    e_core = send(r.e, r.es.at[m.place], r.link_sem, (4,), m.core_peer)
+    e_y = send(r.e_hbm, r.es.at[m.place], r.link_sem, (3,), m.y_peer)
+    e_core = send(r.e_hbm, r.es.at[m.place], r.link_sem, (4,), m.core_peer)
     e_on = send(r.es.at[m.across], r.es.at[m.across], r.link_sem, (5,), m.core_peer)
     x_y.start()
     x_core.start()
     e_core.start()
-    r.xs[m.place] = r.x[...]
-    r.es[m.place] = r.e[...]
 
     gain_self = r.gain_self[...].astype(F32).reshape(1, width)
     gain_cross = r.gain_cross[...].astype(F32).reshape(1, width)
@@ -280,6 +281,8 @@
         @pl.when(k == 2)
         def _():
             loads.wout.wait()
+            loads.go.wait()
+            loads.e.wait()
             lax.fori_loop(0, fan, inner_grad, 0)
             loads.cwk.wait()
             loads.cwv.wait()
@@ -301,6 +304,7 @@
 
         return carry
 
+    loads.x.wait()
     loads.wk.wait()
     loads.wv.wait()
     lax.fori_loop(0, 4, self_blocks, 0)
@@ -315,6 +319,8 @@
         keep(r.values, r.values_out, 1),
         keep(r.a1, r.a1_out, 2),
         keep(r.inner_grad, r.inner_out, 6),
+        keep(r.queries_t, r.queries_t_out, 7),
+        keep(r.xs.at[m.across], r.across_out, 14),
     ]
 
     def probs_copy(slot, out, pair):
@@ -349,7 +355,7 @@
     )
     loads.wo.wait()
     context = jnp.transpose(r.context_t[...]).astype(LOW)
-    first = r.x[...].astype(F32) + dot(context, r.wo[...])
+    first = r.xs[m.place].astype(F32) + dot(context, r.wo[...])
     r.first[...] = first
     normed_cross = (first * scale_of(first) * gain_cross).astype(LOW)
     r.a2[...] = normed_cross
@@ -360,6 +366,10 @@
         keep(r.ckeys, r.ckeys_out, 3),
         keep(r.cvalues, r.cvalues_out, 4),
         keep(r.es, r.es_out, 5),
+        keep(r.context_t, r.context_t_out, 8),
+        keep(r.first, r.first_out, 9),
+        keep(r.a2, r.a2_out, 10),
+        keep(r.cqueries_t, r.cqueries_t_out, 11),
     ]
     attend(
         True, r.ckeys, r.cvalues_t, r.cross_terms, r.cqueries_t, r.cross_masses, r.ccontext_t,
@@ -367,7 +377,9 @@
     )
     loads.cwo.wait()
     context = jnp.transpose(r.ccontext_t[...]).astype(LOW)
+    kept.append(keep(r.ccontext_t, r.ccontext_t_out, 12))
     r.second[...] = r.first[...] + dot(context, r.cwo[...])
+    kept.append(keep(r.second, r.second_out, 13))
     for slot in range(2):
         probs_copy(slot, r.cross_probs, pairs - 2 + slot).wait()
     for copy in kept:
@@ -398,9 +410,9 @@
     square = (width, width)
     own = (count, width)
     inputs = dict(
-        x=(a.dec_states[0], near),
-        e=(a.enc_states[0], near),
-        go=(a.out_grad[0], near),
+        x_hbm=(a.dec_states[0], far),
+        e_hbm=(a.enc_states[0], far),
+        go_hbm=(a.out_grad[0], far),
         dec_len=(a.dec_lengths, scalars),
         enc_len=(a.enc_lengths, scalars),
         table=(a.position_bias.T, near),
@@ -417,16 +429,17 @@
         cwo_hbm=(a.cross_output, far),
     )
     outputs = dict(
-        first=(own, F32, near),
-        second=(own, F32, near),
+        first_out=(own, F32, far),
+        second_out=(own, F32, far),
         inner_out=((fan, *own), LOW, far),
-        queries_t=((width, count), LOW, near),
-        cqueries_t=((width, count), LOW, near),
-        context_t=((width, count), F32, near),
-        ccontext_t=((width, count), F32, near),
+        across_out=(own, LOW, far),
+        queries_t_out=((width, count), LOW, far),
+        cqueries_t_out=((width, count), LOW, far),
+        context_t_out=((width, count), F32, far),
+        ccontext_t_out=((width, count), F32, far),
         self_masses=((pairs, 1, 2 * count), F32, near),
         cross_masses=((pairs, 1, 2 * count), F32, near),
-        a2=(own, LOW, near),
+        a2_out=(own, LOW, far),
         keys_out=((dims.places, *own), LOW, far),
         values_out=((dims.places, *own), LOW, far),
         a1_out=((dims.places, *own), LOW, far),
@@ -438,6 +451,14 @@
     )
     scratch = dict(
         xs=pltpu.VMEM((dims.places, *own), LOW),
+        go=pltpu.VMEM(own, LOW),
+        first=pltpu.VMEM(own, F32),
+        second=pltpu.VMEM(own, F32),
+        queries_t=pltpu.VMEM((width, count), LOW),
+        cqueries_t=pltpu.VMEM((width, count), LOW),
+        context_t=pltpu.VMEM((width, count), F32),
+        ccontext_t=pltpu.VMEM((width, count), F32),
+        a2=pltpu.VMEM(own, LOW),
         es=pltpu.VMEM((dims.places, *own), LOW),
         wk=pltpu.VMEM(square, LOW),
         wv=pltpu.VMEM(square, LOW),
@@ -461,9 +482,9 @@
         scores=pltpu.VMEM((total, 2 * count), F32),
         probs=pltpu.VMEM((2, total, 2 * count), LOW),
         inner_grad=pltpu.VMEM((fan, *own), LOW),
-        load_sem=pltpu.SemaphoreType.DMA((10,)),
+        load_sem=pltpu.SemaphoreType.DMA((12,)),
         link_sem=pltpu.SemaphoreType.DMA((2, 6)),
-        keep_sem=pltpu.SemaphoreType.DMA((7,)),
+        keep_sem=pltpu.SemaphoreType.DMA((15,)),
         probs_sem=pltpu.SemaphoreType.DMA((2,)),
     )
     return call(
@@ -472,11 +493,11 @@
     )
 
 
-SWAPPED = (1, 4, 6, 8, 10, 13, 16, 19, 22)
+SWAPPED = (1, 4, 7, 10, 12, 13, 16, 19)
 
 
 class Reducer:
-    LAGS = (0, 3, 5, 7, 10, 14)
+    LAGS = (0, 3, 6, 8, 11, 15)
 
     def __init__(self, r, m, dims):
         self.r, self.m = r, m
@@ -512,13 +533,24 @@
             found = found | (index == other)
         return found
 
-    def route(self, index, first, other):
+    def by_halves(self, index):
+        return lax.rem(index, 6) == 3
+
+    def route(self, index, first, other, third=None):
         if not self.line:
             first(index)
             return
         special = self.by_planes(index)
-
-        @pl.when(jnp.logical_not(special))
+        usual = jnp.logical_not(special)
+        if third is not None:
+            early = self.by_halves(index)
+            usual = usual & jnp.logical_not(early)
+
+            @pl.when(early)
+            def _():
+                third(index)
+
+        @pl.when(usual)
         def _():
             first(index)
 
@@ -645,7 +677,10 @@
         for side in range(2):
             r.sums[side, rows, :] = add_low(r.sums[side, rows, :], r.fresh[side, fresh, :])
         self.route(
-            index, lambda at: self.y_copy(at).start(), lambda at: self.swap_copy(at).start()
+            index,
+            lambda at: self.y_copy(at).start(),
+            lambda at: self.swap_copy(at).start(),
+            lambda at: self.early_copy(at).start(),
         )
 
         if not prefetch:
@@ -657,8 +692,8 @@
 
     def move(self, step):
         stages = (
-            (self.after_y, self.after_swap),
-            (self.after_x, self.swapped_y),
+            (self.after_y, self.after_swap, self.after_early),
+            (self.after_x, self.swapped_y, self.early_y),
             (self.inward, self.swapped_x),
             (self.middle, self.swapped_pair),
             (self.outward, self.swapped_back),
@@ -670,6 +705,39 @@
             @pl.when((index >= 0) & (index < self.chunks))
             def _():
                 self.route(index, *stage)
+
+
+    def early_rows(self, index):
+        return self.span(index // 6 * self.half_rows, self.half_rows)
+
+    def early_copy(self, index):
+        r = self.r
+        return send(
+            r.sums.at[:, self.half_of(index, 1 - self.half)],
+            r.early_recv.at[:, self.early_rows(index)],
+            r.x_sem, (index,), self.x_peer,
+        )
+
+    def early_y_copy(self, index):
+        r, rows = self.r, self.half_of(index, self.half)
+        return send(
+            r.sums.at[1 - self.m.side, rows], r.fin.at[rows], r.y_sem, (index,), self.m.y_peer
+        )
+
+    def after_early(self, index):
+        r = self.r
+        self.early_copy(index).wait()
+        rows, packed = self.half_of(index, self.half), self.early_rows(index)
+        for side in range(2):
+            r.sums[side, rows, :] = add_low(r.sums[side, rows, :], r.early_recv[side, packed, :])
+        self.early_y_copy(index).start()
+
+    def early_y(self, index):
+        r, m = self.r, self.m
+        self.early_y_copy(index).wait()
+        rows = self.half_of(index, self.half)
+        r.sums[m.side, rows, :] = add_low(r.sums[m.side, rows, :], r.fin[rows, :])
+        self.give_in(index)
 
 
     def parity(self):
@@ -779,6 +847,9 @@
             for step in range(1, self.planes):
                 self.z_copy(index, step).start()
             return
+        self.give_in(index)
+
+    def give_in(self, index):
         for outer, inner in ((0, 1), (3, 2)):
             @pl.when(self.plane == outer)
             def _():
@@ -987,11 +1058,11 @@
 
 FFN_FEEDS = 3
 PLAN = (
-    (0, 0), (0, 0), (3, 1), (2, 1), (0, 2), (1, 0),
-    (0, 3), (3, 2), (27, 6), (3, 0), (19, 1),
+    (0, 0), (4, 0), (0, 2), (10, 0), (4, 3), (7, 0),
+    (0, 1), (2, 0), (21, 6), (19, 0), (32, 5),
 )
-TAIL_FEEDS = 1
-TAIL = (3, 6, 15, 19, 31)
+TAIL_FEEDS = 2
+TAIL = (2, 9, 13, 15, 24, 7, 38)
 
 
 def backward_kernel(names, dims, *refs):
@@ -1021,6 +1092,7 @@
 
     third = width // count
     loads.second = load(r.second_hbm, r.second)
+    loads.go = load(r.go_hbm, r.go)
 
     def ffn_copies(index):
         rows = pl.ds(index * third, third)
@@ -1045,6 +1117,7 @@
     loads.queries = load(r.queries_hbm, r.queries_t)
     loads.context = load(r.context_hbm, r.context_t)
     loads.a2 = load(r.a2_hbm, r.a2)
+    loads.x = load(r.x_hbm, r.x)
 
     m.greet([m.core_peer, m.y_peer] + engine.peers())
 
@@ -1139,6 +1212,7 @@
     loads.ckeys, loads.cvalues = later(r.ckeys_hbm, r.keys), later(r.cvalues_hbm, r.values)
     freed = ((loads.cwo,), (loads.cwq, loads.ckeys), (loads.cwk, loads.cvalues), (loads.cwv,))
     loads.inner.wait()
+    loads.go.wait()
 
     def head_copy(index):
         return pltpu.make_async_copy(
@@ -1236,6 +1310,7 @@
     r.tiny[0, 1:2] = gain_cross_grad
     loads.a2.wait()
     r.query_grad_t[...] = jnp.transpose(r.a2[...])
+    loads.across = load(r.across_hbm, r.a2)
     give(1, r.query_grad_t, query_grad)
     engine.run(*next(plan))
     loads.es0.wait()
@@ -1274,6 +1349,7 @@
     turn(r.keys, r.keys_t)
     loads.values.wait()
     loads.queries.wait()
+    loads.x.wait()
 
     r.by_distance[...] = jnp.zeros_like(r.by_distance)
     attend(r.self_probs, r.queries_t, r.self_masses, r.context_t, r.grad_t, m.place)
@@ -1296,10 +1372,17 @@
     loads.wv.wait()
     enc_copy.wait()
     r.enc_grad[...] += r.partial_recv[0].astype(F32)
-    r.partial_low[...] = partial(1, 1 - m.side).astype(LOW)
+    def gain_part(states, grad):
+        return jnp.sum(grad * states * scale_of(states), axis=0, keepdims=True)
+
+    loads.across.wait()
+    theirs = partial(1, 1 - m.side)
+    r.partial_low[...] = theirs.astype(LOW)
     dec_copy = send(r.partial_low, r.partial_recv.at[1], r.link_sem, (1,), m.y_peer)
-    dec_copy.start()
+    gain_self_grad = gain_part(r.a2[...].astype(F32), theirs)
     normed_grad = normed_grad + partial(1, m.side)
+    gain_self_grad = gain_self_grad + gain_part(r.x[...].astype(F32), normed_grad)
+    r.tiny[0, 0:1] = gain_self_grad
     give(6, r.group_t, key_grad)
     give(7, r.group_t, value_grad)
     settle(4 * width)
@@ -1326,14 +1409,15 @@
     def states():
         dec_copy.wait()
         normed_grad = r.second[...] + r.partial_recv[1].astype(F32)
-        state_part, gain_self_grad = norm_back(r.x[...].astype(F32), gain_self, normed_grad)
+        state_part, _ = norm_back(r.x[...].astype(F32), gain_self, normed_grad)
         r.dec_grad[...] += state_part
+
+    def smalls():
         buckets = dims.buckets
         table = lax.dot_general(
             bucket_terms(buckets), r.by_distance[...], (((1,), (1,)), ((), ())),
             precision=lax.Precision.HIGHEST, preferred_element_type=F32,
         )
-        r.tiny[0, 0:1] = gain_self_grad
         part = buckets // places
         for place in range(places):
             r.tiny[0, 8 : 8 + part, 128 * place : 128 * (place + 1)] = table[
@@ -1348,7 +1432,9 @@
             total = total + r.tiny_recv[2 + step]
         r.small[...] = total
 
-    steps = (states, lambda: arrive(0), lambda: arrive(1), lambda: arrive(2), totals)
+    steps = (
+        smalls, lambda: arrive(0), lambda: arrive(1), lambda: arrive(2), totals, dec_copy.start, states,
+    )
     engine.finish_all(TAIL_FEEDS, tuple(zip(TAIL, steps)))
 
 
@@ -1359,23 +1445,24 @@
     square = (width, width)
     own = (count, width)
     inputs = dict(
-        x=(a.dec_states[0], near),
-        go=(a.out_grad[0], near),
+        x_hbm=(a.dec_states[0], far),
+        go_hbm=(a.out_grad[0], far),
         gain_self=(a.gain_self, near),
         gain_cross=(a.gain_cross, near),
         gain_ffn=(a.gain_ffn, near),
         self_masses=(f.self_masses, near),
         cross_masses=(f.cross_masses, near),
-        first_hbm=(f.first, far),
-        second_hbm=(f.second, far),
+        first_hbm=(f.first_out, far),
+        second_hbm=(f.second_out, far),
         inner_hbm=(f.inner_out, far),
         win_hbm=(a.ffn_in, far),
         wout_hbm=(a.ffn_out.reshape(-1, *own), far),
-        queries_hbm=(f.queries_t, far),
-        cqueries_hbm=(f.cqueries_t, far),
-        context_hbm=(f.context_t, far),
-        ccontext_hbm=(f.ccontext_t, far),
-        a2_hbm=(f.a2, far),
+        queries_hbm=(f.queries_t_out, far),
+        cqueries_hbm=(f.cqueries_t_out, far),
+        context_hbm=(f.context_t_out, far),
+        ccontext_hbm=(f.ccontext_t_out, far),
+        a2_hbm=(f.a2_out, far),
+        across_hbm=(f.across_out, far),
         keys_hbm=(f.keys_out, far),
         values_hbm=(f.values_out, far),
         a1_hbm=(f.a1_out, far),
@@ -1411,6 +1498,8 @@
         probs=pltpu.VMEM((2, total, 2 * count), LOW),
         grad_t=pltpu.VMEM((width, count), LOW),
         a3=pltpu.VMEM(own, LOW),
+        x=pltpu.VMEM(own, LOW),
+        go=pltpu.VMEM(own, LOW),
         a2=pltpu.VMEM(own, LOW),
         queries_t=pltpu.VMEM((width, count), LOW),
         cqueries_t=pltpu.VMEM((width, count), LOW),
@@ -1430,6 +1519,9 @@
         fresh=pltpu.VMEM((2, dims.ring * dims.chunk_rows, width), LOW),
         sums=pltpu.VMEM((2, rows, width), LOW),
         x_recv=pltpu.VMEM((rows // 2, width), LOW),
+        early_recv=pltpu.VMEM(
+            (2, -(-dims.chunks // 6) * dims.chunk_rows // 2 if dims.line else dims.piece, width), LOW
+        ),
         z_recv=pltpu.VMEM(
             (2, rows // 2, width) if dims.line else (planes - 1, chunks * piece, width), LOW
         ),

time: 194 us -> 191 us (0.985)
  Pallas kernels: 193 us -> 190 us
    pallas_call x2, Pallas kernels: 186 us -> 182 us  [call(): pl.pallas_call(functools.partial(kernel, names), out_shape=tuple((jax.Sha...]
where the time goes in v1:
time: 191 us
  Pallas kernels  190 us (99%)
    pallas_call x2, Pallas kernels, call(): pl.pallas_call(functools.partial(kernel, names), out_shape=tuple((jax.Sha...  182 us
    pallas_call x1, Pallas kernels, run_place(): pl.pallas_call(lambda *refs: place_kernel(names, dims, *refs), out_shape=...  7.41 us

profile of v1, /device:TPU:0, one launch (start us, length us, event | category | flops | bytes accessed | tf_op | source)
XLA Modules:
  0.0 190.7 jit_solution(14184090481008555438)
XLA Ops:
  0.7 38.1 %forward.1 = (f32[256,768]{1,0:T(8,128)}, f32[256,768]{1,0:T(8,128)}, bf16[4,256,768]{2,1,0:T(8,128)(2,1)}, bf16[256,768]{1,0:T(8,128)(2,1)}, bf16[768,256]{1,0:...) custom-call(bf16[256,768]{1,0:T(8,128)(2,1)} %bitcast.12, ...), custom_call_target="tpu_custom_call" | custom-call | tf_op jit(solution)/shard_map/forward/pallas_call | solution.py:391
  38.8 144.3 %backward.1 = (bf16[2,2,3072,768]{3,2,1,0:T(8,128)(2,1)}, bf16[256,768]{1,0:T(8,128)(2,1)}, bf16[3072,768]{1,0:T(8,128)(2,1)}, f32[256,768]{1,0:T(8,128)}, f32[256,768]{1,0:T(8,128)}, /*index=5*/f32[16,768]{1,0:T(8,128)}) custom-call(bf16[256,768]{1,0:T(8,128)(2,1)} %bitcast.13, bf16[256,768]{1,0:T(8,128)(2,1)} %bitcast.15, bf16[768]{0:T(1024)(128)(2,1)} %refs_2_.1, ...), custom_call_target="tpu_custom_call" | custom-call | tf_op jit(solution)/shard_map/backward/pallas_call | solution.py:391
  183.1 7.4 %place.1 = (bf16[256,768]{1,0:T(8,128)(2,1)}, f32[256,768]{1,0:T(8,128)}, f32[256,768]{1,0:T(8,128)}, f32[768,768]{1,0:T(8,128)}, f32[192,3072]{1,0:T(8,128)}, /...) custom-call(bf16[3072,768]{1,0:T(8,128)(2,1)} %get-tuple-element.77., ...), custom_call_target="tpu_custom_call" | custom-call | tf_op jit(solution)/shard_map/place/pallas_call | solution.py:1653

commit v2 on v1

--- a/solution.py
+++ b/solution.py
@@ -493,11 +493,11 @@
     )
 
 
-SWAPPED = (1, 4, 7, 10, 12, 13, 16, 19)
+SWAPPED = (1, 4, 5, 7, 10, 11, 13, 16, 19)
 
 
 class Reducer:
-    LAGS = (0, 3, 6, 8, 11, 15)
+    LAGS = (0, 4, 7, 9, 12, 19)
 
     def __init__(self, r, m, dims):
         self.r, self.m = r, m
@@ -1058,11 +1058,11 @@
 
 FFN_FEEDS = 3
 PLAN = (
-    (0, 0), (4, 0), (0, 2), (10, 0), (4, 3), (7, 0),
-    (0, 1), (2, 0), (21, 6), (19, 0), (32, 5),
+    (0, 0), (6, 0), (2, 5), (14, 0), (19, 0), (17, 3),
+    (0, 1), (1, 0), (36, 6), (21, 1), (44, 23),
 )
-TAIL_FEEDS = 2
-TAIL = (2, 9, 13, 15, 24, 7, 38)
+TAIL_FEEDS = 4
+TAIL = (3, 8, 13, 16, 21, 9, 27)
 
 
 def backward_kernel(names, dims, *refs):

time: 191 us -> 190 us (level)
  no operation moved by 1% of the time
where the time goes in v2:
time: 190 us
  Pallas kernels  189 us (99%)
    pallas_call x2, Pallas kernels, call(): pl.pallas_call(functools.partial(kernel, names), out_shape=tuple((jax.Sha...  181 us
    pallas_call x1, Pallas kernels, run_place(): pl.pallas_call(lambda *refs: place_kernel(names, dims, *refs), out_shape=...  7.41 us

profile of v2, /device:TPU:0, one launch (start us, length us, event | category | flops | bytes accessed | tf_op | source)
XLA Modules:
  0.0 189.7 jit_solution(17269038041710359041)
XLA Ops:
  0.7 38.1 %forward.1 = (f32[256,768]{1,0:T(8,128)}, f32[256,768]{1,0:T(8,128)}, bf16[4,256,768]{2,1,0:T(8,128)(2,1)}, bf16[256,768]{1,0:T(8,128)(2,1)}, bf16[768,256]{1,0:...) custom-call(bf16[256,768]{1,0:T(8,128)(2,1)} %bitcast.12, ...), custom_call_target="tpu_custom_call" | custom-call | tf_op jit(solution)/shard_map/forward/pallas_call | solution.py:391
  38.8 143.3 %backward.1 = (bf16[2,2,3072,768]{3,2,1,0:T(8,128)(2,1)}, bf16[256,768]{1,0:T(8,128)(2,1)}, bf16[3072,768]{1,0:T(8,128)(2,1)}, f32[256,768]{1,0:T(8,128)}, f32[256,768]{1,0:T(8,128)}, /*index=5*/f32[16,768]{1,0:T(8,128)}) custom-call(bf16[256,768]{1,0:T(8,128)(2,1)} %bitcast.13, bf16[256,768]{1,0:T(8,128)(2,1)} %bitcast.15, bf16[768]{0:T(1024)(128)(2,1)} %refs_2_.1, ...), custom_call_target="tpu_custom_call" | custom-call | tf_op jit(solution)/shard_map/backward/pallas_call | solution.py:391
  182.1 7.4 %place.1 = (bf16[256,768]{1,0:T(8,128)(2,1)}, f32[256,768]{1,0:T(8,128)}, f32[256,768]{1,0:T(8,128)}, f32[768,768]{1,0:T(8,128)}, f32[192,3072]{1,0:T(8,128)}, /...) custom-call(bf16[3072,768]{1,0:T(8,128)(2,1)} %get-tuple-element.77., ...), custom_call_target="tpu_custom_call" | custom-call | tf_op jit(solution)/shard_map/place/pallas_call | solution.py:1653

commit v3 on v2

--- a/solution.py
+++ b/solution.py
@@ -93,11 +93,18 @@
         self.core_peer = (self.row, self.sibling)
         self.y_peer = (self.row, self.across)
 
+    def call_out(self, peers):
+        for peer in peers:
+            pl.semaphore_signal(
+                pltpu.get_barrier_semaphore(), inc=1, device_id=peer, device_id_type=MESH
+            )
+
+    def hear(self, peers):
+        pl.semaphore_wait(pltpu.get_barrier_semaphore(), len(peers))
+
     def greet(self, peers):
-        barrier = pltpu.get_barrier_semaphore()
-        for peer in peers:
-            pl.semaphore_signal(barrier, inc=1, device_id=peer, device_id_type=MESH)
-        pl.semaphore_wait(barrier, len(peers))
+        self.call_out(peers)
+        self.hear(peers)
 
 
 def send(src, dst, sems, slot, peer):
@@ -1119,7 +1126,8 @@
     loads.a2 = load(r.a2_hbm, r.a2)
     loads.x = load(r.x_hbm, r.x)
 
-    m.greet([m.core_peer, m.y_peer] + engine.peers())
+    peers = [m.core_peer, m.y_peer] + engine.peers()
+    m.call_out(peers)
 
     gain_self = r.gain_self[...].astype(F32).reshape(1, width)
     gain_cross = r.gain_cross[...].astype(F32).reshape(1, width)
@@ -1258,6 +1266,11 @@
                 for copy in copies:
                     copy.start()
         tail.wait()
+
+        @pl.when(index == 0)
+        def _():
+            m.hear(peers)
+
         chunk_rows = engine.chunk_rows
         engine.publish_part(index * own // chunk_rows, (index + 1) * own // chunk_rows)
 

time: 190 us -> 190 us (level)
  no operation moved by 1% of the time
where the time goes in v3:
time: 190 us
  Pallas kernels  189 us (99%)
    pallas_call x2, Pallas kernels, call(): pl.pallas_call(functools.partial(kernel, names), out_shape=tuple((jax.Sha...  181 us
    pallas_call x1, Pallas kernels, run_place(): pl.pallas_call(lambda *refs: place_kernel(names, dims, *refs), out_shape=...  7.41 us

profile of v3, /device:TPU:0, one launch (start us, length us, event | category | flops | bytes accessed | tf_op | source)
XLA Modules:
  0.0 189.7 jit_solution(8304294528436903561)
XLA Ops:
  0.7 38.1 %forward.1 = (f32[256,768]{1,0:T(8,128)}, f32[256,768]{1,0:T(8,128)}, bf16[4,256,768]{2,1,0:T(8,128)(2,1)}, bf16[256,768]{1,0:T(8,128)(2,1)}, bf16[768,256]{1,0:...) custom-call(bf16[256,768]{1,0:T(8,128)(2,1)} %bitcast.12, ...), custom_call_target="tpu_custom_call" | custom-call | tf_op jit(solution)/shard_map/forward/pallas_call | solution.py:398
  38.8 143.3 %backward.1 = (bf16[2,2,3072,768]{3,2,1,0:T(8,128)(2,1)}, bf16[256,768]{1,0:T(8,128)(2,1)}, bf16[3072,768]{1,0:T(8,128)(2,1)}, f32[256,768]{1,0:T(8,128)}, f32[256,768]{1,0:T(8,128)}, /*index=5*/f32[16,768]{1,0:T(8,128)}) custom-call(bf16[256,768]{1,0:T(8,128)(2,1)} %bitcast.13, bf16[256,768]{1,0:T(8,128)(2,1)} %bitcast.15, bf16[768]{0:T(1024)(128)(2,1)} %refs_2_.1, ...), custom_call_target="tpu_custom_call" | custom-call | tf_op jit(solution)/shard_map/backward/pallas_call | solution.py:398
  182.1 7.4 %place.1 = (bf16[256,768]{1,0:T(8,128)(2,1)}, f32[256,768]{1,0:T(8,128)}, f32[256,768]{1,0:T(8,128)}, f32[768,768]{1,0:T(8,128)}, f32[192,3072]{1,0:T(8,128)}, /...) custom-call(bf16[3072,768]{1,0:T(8,128)(2,1)} %get-tuple-element.77., ...), custom_call_target="tpu_custom_call" | custom-call | tf_op jit(solution)/shard_map/place/pallas_call | solution.py:1666
